TPU v7x, 32 devices: a whole 2x2x4 slice. The times are simulated.
32 devices in a mesh: pairs: 2 (over y), src: 8 (over z, x), tgt: 2 (over core).
Axes of the slice: x: 2, y: 2, z: 4, core: 2. Of those that a mesh axis runs over, the one named last changes fastest.
Arguments:
- source_expr: bfloat16 [20480, 1024], P('src', 'pairs'), parts along dimension 1, may hold values from -6 to 6
- target_expr: bfloat16 [20480, 8192], P('src', 'pairs'), parts along dimension 1, may hold values from -6 to 6
- loadings: bfloat16 [20480, 50], P('src'), may hold values from -0.0390625 to 0.0390625
- panel: int32 [96], replicated, may hold values from 0 to 20479
- time_label: int32 [1024], P(('pairs', 'src')), parts along dimension 0, may hold values from 0 to 3
- target_order: int32 [8192], P('pairs'), parts along dimension 0, may hold values from 0 to 4095, each once
Outputs:
- coupling: float32 [1024, 4096], P(('pairs', 'src'), 'tgt'), parts along dimension 0
There are 2 independent parts, one for each index of `pairs`. A program takes and returns all parts, laid end to end along the dimension named above; an argument that names none is the same for every part. Nothing has to cross between parts.
Inputs may be any that keep to these rules, and one draw needn't show every extreme that they name: `panel`: each entry is the index of a gene. `target_order`: a permutation of the target cells.
All inputs are finite; a program needn't handle non-finite values.
Results may differ from a plain program's by a relative error of at most 0.0003.
Values sent between devices are 32-bit elements; how exact they have to be, the bound alone decides.
A program may use at most 128 MiB of HBM per device.

v0:
```python
import jax
import jax.numpy as jnp
from jax import lax
from jax.sharding import PartitionSpec as P

LEVELS = 4
ITERS = 3


def gene_sum(left, right):
    return lax.dot_general(
        left, right, (((0,), (0,)), ((), ())), preferred_element_type=jnp.float32
    )


def build_kernel(source_pc, target_pc, mean_d2):
    src_sq = jnp.sum(source_pc * source_pc, axis=0)
    tgt_sq = jnp.sum(target_pc * target_pc, axis=0)
    cross = lax.dot_general(
        source_pc, target_pc, (((0,), (0,)), ((), ())), precision=lax.Precision.HIGHEST
    )
    d2 = src_sq[:, None] + tgt_sq[None, :] - 2.0 * cross
    return jnp.exp(-(d2 / mean_d2) / 0.1)


def local(source_expr, target_expr, loadings, panel, time_label, target_order):
    genes = source_expr.shape[0]
    first_gene = lax.axis_index("src") * genes
    gene_ids = first_gene + lax.broadcasted_iota(jnp.int32, (genes, panel.shape[0]), 0)
    counts = jnp.sum((gene_ids == panel[None, :]).astype(jnp.float32), axis=1).astype(jnp.bfloat16)
    source_pc = lax.psum_scatter(
        gene_sum(loadings, source_expr), "src", scatter_dimension=1, tiled=True
    )
    score_part = jnp.dot(counts[None, :], source_expr, preferred_element_type=jnp.float32)
    score_raw = lax.psum_scatter(score_part, "src", scatter_dimension=1, tiled=True)[0]
    score = score_raw / jnp.sqrt(jnp.float32(panel.shape[0]))
    total_targets = target_expr.shape[1]
    total_sources = source_expr.shape[1]
    columns = total_targets // lax.axis_size("tgt")
    local_order = lax.dynamic_slice_in_dim(target_order, lax.axis_index("tgt") * columns, columns)
    target_all = lax.psum(gene_sum(loadings, target_expr), "src")
    target_pc = jnp.take(target_all, local_order, axis=1)
    src_share = 1.0 / jnp.float32(lax.axis_size("tgt"))
    tgt_share = 1.0 / jnp.float32(lax.axis_size("src"))
    src_sq_sum, src_vec, tgt_sq_sum, tgt_vec = lax.psum(
        (
            jnp.sum(source_pc * source_pc) * src_share,
            jnp.sum(source_pc, axis=1) * src_share,
            jnp.sum(target_pc * target_pc) * tgt_share,
            jnp.sum(target_pc, axis=1) * tgt_share,
        ),
        ("src", "tgt"),
    )
    src_mean = src_vec / jnp.float32(total_sources)
    tgt_mean = tgt_vec / jnp.float32(total_targets)
    mean_d2 = (
        src_sq_sum / jnp.float32(total_sources)
        + tgt_sq_sum / jnp.float32(total_targets)
        - 2.0 * jnp.sum(src_mean * tgt_mean)
    )
    spans = 0.5 * (jnp.float32(LEVELS) - time_label.astype(jnp.float32))
    growth = jnp.exp(spans * jnp.clip(score, -2.0, 2.0))
    target_mass = jnp.float32(total_sources) / jnp.float32(total_targets)
    power = 1.0 / 1.1
    stored = build_kernel(source_pc, target_pc, mean_d2)
    scale_v = jnp.ones((columns,), jnp.float32)
    scale_u = jnp.ones((source_pc.shape[1],), jnp.float32)
    for step in range(ITERS):
        row_part = jnp.dot(stored, scale_v, precision=lax.Precision.HIGHEST)
        scale_u = (growth / lax.psum(row_part, "tgt")) ** power
        col_part = jnp.dot(scale_u, stored, precision=lax.Precision.HIGHEST)
        scale_v = (target_mass / lax.psum(col_part, "src")) ** power
    return jnp.float32(total_targets) * scale_u[:, None] * stored * scale_v[None, :]


def solution(mesh):
    return jax.shard_map(
        local,
        mesh=mesh,
        in_specs=(
            P("src", "pairs"),
            P("src", "pairs"),
            P("src", None),
            P(),
            P(("pairs", "src")),
            P("pairs"),
        ),
        out_specs=P(("pairs", "src"), "tgt"),
        check_vma=False,
    )
```

profile of v0, /device:TPU:0, one launch (start us, length us, event | category | flops | bytes accessed | tf_op | source)
XLA Modules:
  0.0 340.6 jit_solution(8237559134335003328)
XLA Ops:
  6.5 1.0 convert_reduce_fusion
  7.6 0.7 copy-done
  8.3 1.8 convolution_bitcast_fusion.1
  10.2 1.8 convolution_bitcast_fusion
  12.1 9.8 %fusion.30 = f32[50,4096]{1,0:T(8,128)} fusion(bf16[2560,50]{0,1:T(8,128)(2,1)S(1)} %copy-done.1, bf16[2560,4096]{1,0:T(8,128)(2,1)} %param.7), kind=kOutput, calls=%fused_computation.56 | convolution fusion | flops 1048576000 | bytes 22046720 | tf_op jit(solution)/shard_map/dot_general | solution.py:11
  22.0 52.7 %reduce-scatter.7.cloned.1.call-done = f32[64,1]{1,0:T(8,128)} async-done(((f32[512,1]{1,0:T(8,128)}), f32[64,1]{1,0:T(8,128)}) %reduce-scatter.7.cloned.1.call-update) | async-done | bytes 272
  74.7 0.8 clamp_bitcast_fusion
  75.5 63.2 %reduce-scatter.9.cloned.1.call-done = f32[64,50]{1,0:T(8,128)} async-done(((f32[512,50]{1,0:T(8,128)}), f32[64,50]{1,0:T(8,128)}) %reduce-scatter.9.cloned.1.call-update) | async-done | bytes 12816
  138.7 0.8 copy.13
  139.5 0.6 multiply_reduce_fusion.3
  140.8 0.8 bitcast_reduce_fusion
  141.6 76.1 %all-reduce.3.cloned.1.call-done = f32[50,4096]{1,0:T(8,128)} async-done(((f32[50,4096]{1,0:T(8,128)}), f32[50,4096]{1,0:T(8,128)}) %all-reduce.3.cloned.1.call-update) | async-done | bytes 819216 | tf_op jit(solution)/shard_map/psum | solution.py:41
  217.7 3.2 copy.9
  220.9 9.1 %gather_fusion = f32[2048,50]{1,0:T(8,128)} fusion(f32[50,4096]{0,1:T(8,128)} %copy.9, s32[2048]{0:T(1024)S(1)} %fusion.8), kind=kCustom, calls=%fused_computation | custom fusion | bytes 827392 | tf_op jit(solution)/shard_map/jit(_take)/gather | solution.py:42
  230.0 2.4 multiply_reduce_fusion
  233.1 30.5 %all-reduce = (f32[]{:T(128)}, f32[]{:T(128)}, f32[50]{0:T(128)S(1)}, f32[50]{0:T(128)S(1)}) all-reduce(f32[]{:T(128)S(6)} %mul.85, f32[]{:T(128)S(6)} %mul.86, f32[50]{0:T(128)S(1)} %broadcast_multiply_fusion.1, f32[50]{0:T(128)S(1)} %broadcast_multiply_fusion.2), channel_id=1, replica_groups=mesh['pairs'=2,'src'=8,'tgt'=2] {'src','tgt'}, use_global_device_ids=true, to_apply=%region_7.8 | all-reduce | flops 102 | bytes 816 | tf_op jit(solution)/shard_map/psum | solution.py:45
  266.1 2.7 fusion.4
  269.4 2.5 psum.82
  272.2 17.4 %psum.83 = f32[2048]{0:T(1024)S(1)} all-reduce(f32[2048]{0:T(1024)S(1)} %bitcast.60), channel_id=1, replica_groups=mesh['pairs'=2,'src'=8,'tgt'=2] {'src'}, use_global_device_ids=true, to_apply=%region_16.17 | all-reduce | flops 2048 | bytes 16384 | tf_op jit(solution)/shard_map/psum | solution.py:72
  290.1 2.5 psum.84
  292.9 19.4 %psum.85 = f32[2048]{0:T(1024)S(1)} all-reduce(f32[2048]{0:T(1024)S(1)} %bitcast.62), channel_id=1, replica_groups=mesh['pairs'=2,'src'=8,'tgt'=2] {'src'}, use_global_device_ids=true, to_apply=%region_18.19 | all-reduce | flops 2048 | bytes 16384 | tf_op jit(solution)/shard_map/psum | solution.py:72
  312.9 2.5 psum.86
  315.8 17.4 %psum.87 = f32[2048]{0:T(1024)S(1)} all-reduce(f32[2048]{0:T(1024)S(1)} %bitcast.64), channel_id=1, replica_groups=mesh['pairs'=2,'src'=8,'tgt'=2] {'src'}, use_global_device_ids=true, to_apply=%region_20.21 | all-reduce | flops 2048 | bytes 16384 | tf_op jit(solution)/shard_map/psum | solution.py:72
  333.2 0.9 multiply_multiply_fusion
  (33 shorter events, 3.6 us)
Async XLA Ops:
  6.5 1.8 copy-start
  6.5 3.7 %copy-start.1 = (bf16[2560,50]{0,1:T(8,128)(2,1)S(1)}, bf16[2560,50]{0,1:T(8,128)(2,1)}, u32[]{:S(2)}) copy-start(bf16[2560,50]{0,1:T(8,128)(2,1)} %param.8) | copy-start | bytes 768004
  6.5 68.2 %reduce-scatter.7.cloned.1.call-start = ((), (), s32[]{:S(2)}) async-start(), calls=%async_computation.3 | async-start | bytes 294912
  10.1 128.5 %reduce-scatter.9.cloned.1.call-start = ((), (), s32[]{:S(2)}) async-start(), calls=%async_computation.4 | async-start | bytes 294912
  12.1 9.9 %copy-start.3 = (s32[4096]{0:T(1024)S(1)}, s32[4096]{0:T(1024)}, u32[]{:S(2)}) copy-start(s32[4096]{0:T(1024)} %param.11) | copy-start | bytes 49156
  12.1 205.6 %all-reduce.3.cloned.1.call-start = ((), (), s32[]{:S(2)}) async-start(), calls=%async_computation.2 | async-start | bytes 1835008 | tf_op jit(solution)/shard_map/psum | solution.py:41
  220.9 45.3 %copy-start.2 = (f32[64,50]{1,0:T(8,128)S(1)}, f32[64,50]{1,0:T(8,128)}, u32[]{:S(2)}) copy-start(f32[64,50]{1,0:T(8,128)} %reduce-scatter.9.cloned.1.call-done) | copy-start | bytes 38404
  230.0 41.8 %copy-start.4 = (s32[64]{0:T(128)S(1)}, s32[64]{0:T(128)}, u32[]{:S(2)}) copy-start(s32[64]{0:T(128)} %param.10) | copy-start | bytes 772
Sparse Core Ops, SparseCore 0:
  10.7 63.9 reduce-scatter.6
  78.0 60.5 reduce-scatter.8
  142.2 75.4 all-reduce.2
where the time goes:
time: 341 us
  waiting for transfers between devices  192 us (56%)
  blocking collectives  92.1 us (27%)
  matrix products  18.8 us (6%)
  between operations  16.4 us (5%)
  local copies, waits for them, and re-layouts  14 us (4%)
  other arithmetic  7.15 us (2%)
    unnamed x5, waiting for transfers between devices  116 us
    psum x1, waiting for transfers between devices, local(): target_all = lax.psum(gene_sum(loadings, target_expr), 'src')  76.1 us
    psum x3, blocking collectives, local(): scale_v = (target_mass / lax.psum(col_part, 'src')) ** power  54.2 us
    psum x1, blocking collectives, local(): lax.psum((jnp.sum(source_pc * source_pc) * src_share, jnp.sum(source_pc,...  30.5 us
    dot_general x1, matrix products, gene_sum(): lax.dot_general(left, right, (((0,), (0,)), ((), ())), preferred_element_...  9.79 us
    gather x1, local copies, waits for them, and re-layouts, local(): target_pc = jnp.take(target_all, local_order, axis=1)  9.15 us
    psum x3, blocking collectives, local(): scale_u = (growth / lax.psum(row_part, 'tgt')) ** power  7.38 us
  transfers between devices with their start and end apart: 3, of which 3 were waited for; matrix products, arithmetic and copies ran while one was open for 4% of the time, Pallas kernels for 0%

commit v1 on v0

--- a/solution.py
+++ b/solution.py
@@ -1,6 +1,10 @@
+import functools
+
 import jax
 import jax.numpy as jnp
 from jax import lax
+from jax.experimental import pallas as pl
+from jax.experimental.pallas import tpu as pltpu
 from jax.sharding import PartitionSpec as P
 
 LEVELS = 4
@@ -72,10 +76,327 @@
         scale_v = (target_mass / lax.psum(col_part, "src")) ** power
     return jnp.float32(total_targets) * scale_u[:, None] * stored * scale_v[None, :]
 
+def proj(left, right):
+    return lax.dot_general(left, right, (((1,), (0,)), ((), ())), preferred_element_type=jnp.float32)
+
+
+def proj_nt(left, right, precision=None):
+    return lax.dot_general(
+        left, right, (((1,), (1,)), ((), ())), precision=precision, preferred_element_type=jnp.float32
+    )
+
+
+def exact(left, right):
+    return lax.dot_general(
+        left, right, (((1,), (0,)), ((), ())), precision=lax.Precision.HIGHEST, preferred_element_type=jnp.float32
+    )
+
+
+def power_of(x):
+    return jnp.exp(jnp.log(x) * (1.0 / 1.1))
+
+
+def iota(shape, axis):
+    return lax.broadcasted_iota(jnp.int32, shape, axis)
+
+
+def fused(
+    n, components, source_hbm, target_hbm, load_ref, panel_ref, label_ref, order_ref, out_ref,
+    xs, xt, weights, part_t, recv_t, part_s, recv_s, all_t, all_s, stat, rows, lookup, perm, cols,
+    load_sem, rt_send, rt_recv, rs_send, rs_recv, as_send, as_recv, st_send, st_recv, at_send, at_recv,
+    fw_send, fw_recv, it_send, it_recv, co_send, co_recv,
+):
+    me = lax.axis_index("src")
+    core = lax.axis_index("tgt")
+    slot = core * n + me
+    genes = load_ref.shape[0]
+    width = xt.shape[2]
+    half_s = xs.shape[1]
+    high = recv_t.shape[1]
+    n_targets = target_hbm.shape[1]
+    n_sources = source_hbm.shape[1]
+    own = out_ref.shape[0]
+    columns = out_ref.shape[1]
+    deep = 8 * n
+
+    def peer(d):
+        return lax.rem(me + d, n)
+
+    def remote(src, dst, send, recv, s, c):
+        return pltpu.make_async_remote_copy(
+            src_ref=src, dst_ref=dst, send_sem=send, recv_sem=recv,
+            device_id={"src": s, "tgt": c}, device_id_type=pl.DeviceIdType.MESH,
+        )
+
+    others = [(d, e) for e in range(2) for d in range(n) if (d, e) != (0, 0)]
+
+    turn = [n // 2 + k * sign for k in range(n // 2) for sign in ((1, -1) if k else (1,))] + [0]
+
+    barrier = pltpu.get_barrier_semaphore()
+    for d, e in others:
+        pl.semaphore_signal(
+            barrier, inc=1, device_id={"src": peer(d), "tgt": lax.rem(core + e, 2)},
+            device_id_type=pl.DeviceIdType.MESH,
+        )
+
+    load_s = pltpu.make_async_copy(
+        source_hbm.at[:, pl.ds(pl.multiple_of(core * half_s, 128), half_s)], xs, load_sem.at[n]
+    )
+    load_s.start()
+    loads = []
+    for d in turn:
+        start = pl.multiple_of(core * columns + peer(d) * width, 128)
+        load = pltpu.make_async_copy(target_hbm.at[:, pl.ds(start, width)], xt.at[d], load_sem.at[d])
+        load.start()
+        loads.append(load)
+
+    eye = (iota((deep, components), 0) == iota((deep, components), 1)).astype(jnp.bfloat16)
+    base = proj_nt(eye, load_ref[...])
+    hits = (iota((genes, panel_ref.shape[1]), 0) + me * genes == panel_ref[...]).astype(jnp.float32)
+    pick = (iota((deep, panel_ref.shape[1]), 0) == components).astype(jnp.bfloat16)
+    counts = proj_nt(pick, hits.astype(jnp.bfloat16))
+    weights[0] = base.astype(jnp.bfloat16)
+    weights[1] = (base + counts).astype(jnp.bfloat16)
+
+    spans = 0.5 * (LEVELS - label_ref[...].astype(jnp.float32))
+    place = (iota((own, half_s), 0) + me * own == iota((own, half_s), 1) + core * half_s).astype(jnp.bfloat16)
+    placed = proj(jnp.broadcast_to(spans, (16, own)).astype(jnp.bfloat16), place)[0:1]
+    load_s.wait()
+    source_part = proj(weights[1], xs[...])
+    part_s[...] = jnp.where(iota((deep, half_s), 0) == components + 1, placed, source_part)
+    recv_s[me] = part_s[pl.ds(pl.multiple_of(me * 8, 8), 8), :]
+
+    pl.semaphore_wait(barrier, len(others))
+    sends = []
+
+    def go(copy):
+        copy.start()
+        sends.append(copy)
+
+    for d in turn[:-1]:
+        p = peer(d)
+        go(remote(part_s.at[pl.ds(pl.multiple_of(p * 8, 8), 8)], recv_s.at[me], rs_send.at[d], rs_recv.at[me], p, core))
+
+    for d, load in zip(turn, loads):
+        load.wait()
+        block = proj(weights[0], xt[d])[:high]
+        if d:
+            part_t[d] = block
+            go(remote(part_t.at[d], recv_t.at[me], rt_send.at[d], rt_recv.at[me], peer(d), core))
+        else:
+            recv_t[me] = block
+
+    for d in range(1, n):
+        p = peer(d)
+        remote(recv_s.at[p], recv_s.at[p], rs_send.at[d], rs_recv.at[p], p, core).wait_recv()
+    my_rows = pl.ds(pl.multiple_of(me * 8, 8), 8)
+    my_lanes = pl.ds(pl.multiple_of(core * half_s, 128), half_s)
+    total = recv_s[0]
+    for s in range(1, n):
+        total = total + recv_s[s]
+    all_s[my_rows, my_lanes] = total
+    for q, (d, e) in enumerate(others):
+        c = lax.rem(core + e, 2)
+        here = all_s.at[my_rows, my_lanes]
+        go(remote(here, here, as_send.at[q], as_recv.at[slot], peer(d), c))
+
+    order = order_ref[:, pl.ds(pl.multiple_of(core * columns, 128), columns)]
+    block_of = order // width
+    lookup[...] = (iota((width, columns), 0) == order - block_of * width).astype(jnp.float32).astype(jnp.bfloat16)
+
+    for d in range(1, n):
+        p = peer(d)
+        remote(recv_t.at[p], recv_t.at[p], rt_send.at[d], rt_recv.at[p], p, core).wait_recv()
+    mine = recv_t[0]
+    for s in range(1, n):
+        mine = mine + recv_t[s]
+    all_t[slot] = mine
+    turned = jnp.transpose(jnp.concatenate([mine, jnp.zeros((128 - high, width), jnp.float32)], axis=0))
+    sums = jnp.sum(turned, axis=0, keepdims=True)
+    norms = jnp.sum(turned * turned, axis=1, keepdims=True)
+    stat[slot] = jnp.where(iota((1, 128), 1) == 127, jnp.sum(norms, axis=0, keepdims=True), sums)
+    for q, (d, e) in enumerate(others):
+        c = lax.rem(core + e, 2)
+        go(remote(stat.at[slot], stat.at[slot], st_send.at[q], st_recv.at[slot], peer(d), c))
+    for d in turn:
+        if d:
+            go(remote(all_t.at[slot], all_t.at[slot], at_send.at[d], at_recv.at[me], peer(d), core))
+    go(remote(all_t.at[slot], all_t.at[slot], fw_send.at[0], fw_recv.at[me], me, 1 - core))
+
+    for q, (d, e) in enumerate(others):
+        p, c = peer(d), lax.rem(core + e, 2)
+        there = all_s.at[pl.ds(pl.multiple_of(p * 8, 8), 8), pl.ds(pl.multiple_of(c * half_s, 128), half_s)]
+        remote(there, there, as_send.at[q], as_recv.at[c * n + p], p, c).wait_recv()
+    source = all_s[...]
+    growth = jnp.exp(
+        source[components + 1 : components + 2]
+        * jnp.clip(source[components : components + 1] / jnp.sqrt(jnp.float32(panel_ref.shape[1])), -2.0, 2.0)
+    )
+    pcs = jnp.where(iota(source.shape, 0) < components, source, 0.0)
+    source_sq = jnp.sum(pcs * pcs, axis=0, keepdims=True)
+    cross = exact(turned[:, :deep], pcs)
+    d2 = norms + source_sq - 2.0 * cross
+    mine_hot = (iota((own, n_sources), 0) + me * own == iota((own, n_sources), 1)).astype(jnp.float32)
+    own_pc = proj_nt(mine_hot, pcs, lax.Precision.HIGHEST)
+    own_sq = jnp.sum(own_pc * own_pc, axis=1, keepdims=True)
+
+    for q, (d, e) in enumerate(others):
+        p, c = peer(d), lax.rem(core + e, 2)
+        there = stat.at[c * n + p]
+        remote(there, there, st_send.at[q], st_recv.at[c * n + p], p, c).wait_recv()
+    stats = stat[0]
+    for s in range(1, 2 * n):
+        stats = stats + stat[s]
+    target_sq = jnp.sum(jnp.where(iota((1, 128), 1) == 127, stats, 0.0), axis=1, keepdims=True)
+    dots = exact(jnp.broadcast_to(stats[:, :deep], (8, deep)), pcs)[0:1]
+    mean = (
+        jnp.sum(source_sq, axis=1, keepdims=True) / n_sources
+        + target_sq / n_targets
+        - 2.0 * (jnp.sum(dots, axis=1, keepdims=True) / n_sources / n_targets)
+    )
+    stored = jnp.exp(-(d2 / mean) / 0.1)
+
+    def spread(step, values):
+        rows[step, slot] = values
+        for q, (d, e) in enumerate(others):
+            c = lax.rem(core + e, 2)
+            here = rows.at[step, slot]
+            go(remote(here, here, it_send.at[step, q], it_recv.at[step, slot], peer(d), c))
+
+    def gather(step):
+        for q, (d, e) in enumerate(others):
+            p, c = peer(d), lax.rem(core + e, 2)
+            there = rows.at[step, c * n + p]
+            remote(there, there, it_send.at[step, q], it_recv.at[step, c * n + p], p, c).wait_recv()
+        full = rows[step, 0]
+        for s in range(1, 2 * n):
+            full = full + rows[step, s]
+        return power_of(growth / full)
+
+    def place_blocks(first):
+        @pl.loop(0, n)
+        def _(k):
+            index = first + k
+            block = all_t[index]
+            top = block.astype(jnp.bfloat16).astype(jnp.float32)
+            rest = block - top
+            middle = rest.astype(jnp.bfloat16).astype(jnp.float32)
+            three = jnp.concatenate([top, middle, rest - middle], axis=0).astype(jnp.bfloat16)
+            found = proj(three, lookup[...])
+            found = (found[:high] + found[high : 2 * high]) + found[2 * high :]
+            perm[...] = jnp.where(block_of == index, found, perm[...])
+
+    target_mass = n_sources / n_targets
+    spread(0, jnp.sum(stored, axis=0, keepdims=True))
+    perm[...] = jnp.zeros_like(perm)
+    scale_u = gather(0)
+    scale_v = power_of(target_mass / jnp.sum(stored * scale_u, axis=1, keepdims=True))
+    spread(1, jnp.sum(stored * scale_v, axis=0, keepdims=True))
+    for d in turn[:-1]:
+        p = peer(d)
+        there = all_t.at[core * n + p]
+        remote(there, there, at_send.at[d], at_recv.at[p], p, core).wait_recv()
+        go(remote(there, there, fw_send.at[d], fw_recv.at[p], me, 1 - core))
+    place_blocks(core * n)
+    scale_u = gather(1)
+    scale_v = power_of(target_mass / jnp.sum(stored * scale_u, axis=1, keepdims=True))
+    spread(2, jnp.sum(stored * scale_v, axis=0, keepdims=True))
+    for d in range(n):
+        p = peer(d)
+        there = all_t.at[(1 - core) * n + p]
+        remote(there, there, fw_send.at[d], fw_recv.at[p], me, 1 - core).wait_recv()
+    place_blocks((1 - core) * n)
+    placed_t = perm[...]
+    placed_sq = jnp.sum(placed_t * placed_t, axis=0, keepdims=True)
+    out_ref[...] = jnp.exp(-((own_sq + placed_sq - 2.0 * exact(own_pc[:, :high], placed_t)) / mean) / 0.1)
+    scale_u = gather(2)
+    own_u = jnp.sum(mine_hot * scale_u, axis=1, keepdims=True)
+    cols[me] = jnp.sum(out_ref[...] * own_u, axis=0, keepdims=True)
+    for d in range(1, n):
+        go(remote(cols.at[me], cols.at[me], co_send.at[d], co_recv.at[me], peer(d), core))
+    out_ref[...] = n_targets * own_u * out_ref[...]
+    for d in range(1, n):
+        p = peer(d)
+        remote(cols.at[p], cols.at[p], co_send.at[d], co_recv.at[p], p, core).wait_recv()
+    full = cols[0]
+    for s in range(1, n):
+        full = full + cols[s]
+    out_ref[...] = out_ref[...] * power_of(target_mass / full)
+    for copy in sends:
+        copy.wait_send()
+
+
+def fused_call(source_expr, target_expr, loadings, panel, time_label, target_order):
+    n = lax.axis_size("src")
+    genes, components = loadings.shape
+    n_sources, n_targets = source_expr.shape[1], target_expr.shape[1]
+    own, columns = n_sources // n, n_targets // 2
+    width, half_s = columns // n, n_sources // 2
+    high = (components + 7) // 8 * 8
+    vmem = pl.BlockSpec(memory_space=pltpu.VMEM)
+    any_spec = pl.BlockSpec(memory_space=pl.ANY)
+    dma = pltpu.SemaphoreType.DMA
+    f32 = jnp.float32
+    return pl.pallas_call(
+        functools.partial(fused, n, components),
+        out_shape=jax.ShapeDtypeStruct((own, columns), f32),
+        in_specs=[any_spec, any_spec, vmem, vmem, vmem, vmem],
+        out_specs=vmem,
+        scratch_shapes=[
+            pltpu.VMEM((genes, half_s), jnp.bfloat16),
+            pltpu.VMEM((n, genes, width), jnp.bfloat16),
+            pltpu.VMEM((2, 8 * n, genes), jnp.bfloat16),
+            pltpu.VMEM((n, high, width), f32),
+            pltpu.VMEM((n, high, width), f32),
+            pltpu.VMEM((8 * n, half_s), f32),
+            pltpu.VMEM((n, 8, half_s), f32),
+            pltpu.VMEM((2 * n, high, width), f32),
+            pltpu.VMEM((8 * n, n_sources), f32),
+            pltpu.VMEM((2 * n, 1, 128), f32),
+            pltpu.VMEM((ITERS, 2 * n, 1, n_sources), f32),
+            pltpu.VMEM((width, columns), jnp.bfloat16),
+            pltpu.VMEM((high, columns), f32),
+            pltpu.VMEM((n, 1, columns), f32),
+            dma((n + 1,)),
+            dma((n,)), dma((n,)), dma((n,)), dma((n,)),
+            dma((2 * n,)), dma((2 * n,)), dma((2 * n,)), dma((2 * n,)),
+            dma((n,)), dma((n,)), dma((n,)), dma((n,)),
+            dma((ITERS, 2 * n)), dma((ITERS, 2 * n)),
+            dma((n,)), dma((n,)),
+        ],
+        compiler_params=pltpu.CompilerParams(
+            collective_id=0, has_side_effects=True, vmem_limit_bytes=48 * 1024 * 1024
+        ),
+    )(
+        source_expr, target_expr, loadings,
+        panel.reshape(1, -1), time_label.reshape(1, -1), target_order.reshape(1, -1),
+    )
+
+
+def fits(mesh, source_expr, target_expr, loadings, time_label):
+    n = mesh.shape["src"]
+    components = loadings.shape[1]
+    n_sources, n_targets = source_expr.shape[1], target_expr.shape[1]
+    return (
+        mesh.shape["tgt"] == 2
+        and n % 2 == 0
+        and components + 2 <= 8 * n
+        and 8 * n <= 126
+        and n_sources % 256 == 0
+        and n_targets % (2 * n * 128) == 0
+        and loadings.shape[0] % 128 == 0
+        and loadings.shape[0] * (n_targets + n_sources) <= 32 * 1024 * 1024
+    )
+
 
 def solution(mesh):
+    def per_device(*arrays):
+        if fits(mesh, arrays[0], arrays[1], arrays[2], arrays[4]):
+            return fused_call(*arrays)
+        return local(*arrays)
+
     return jax.shard_map(
-        local,
+        per_device,
         mesh=mesh,
         in_specs=(
             P("src", "pairs"),

time: 341 us -> 54.8 us (0.16)
  waiting for transfers between devices: 192 us -> 0 us
  blocking collectives: 92.1 us -> 0 us
  Pallas kernels: 0 us -> 48.7 us
  matrix products: 18.8 us -> 0 us
  between operations: 16.4 us -> 0.02 us
  local copies, waits for them, and re-layouts: 14 us -> 5.87 us
  other arithmetic: 7.15 us -> 0 us
    unnamed x5 -> x0, waiting for transfers between devices: 116 us -> none
    psum x7 -> x0, blocking collectives: 92.1 us -> none  [the longest x3 54.2 us: local(): scale_v = (target_mass / lax.psum(col_part, 'src')) ** power]
    psum x1 -> x0, waiting for transfers between devices: 76.1 us -> none  [local(): target_all = lax.psum(gene_sum(loadings, target_expr), 'src')]
    pallas_call x0 -> x1, Pallas kernels: none -> 48.7 us  [fused_call(): pl.pallas_call(functools.partial(fused, n, components), out_shape=jax.Sha...]
    dot_general x8 -> x0, matrix products: 15.2 us -> none  [the longest x1 9.79 us: gene_sum(): lax.dot_general(left, right, (((0,), (0,)), ((), ())), preferred_element_...]
    gather x1 -> x0, local copies, waits for them, and re-layouts: 9.15 us -> none  [local(): target_pc = jnp.take(target_all, local_order, axis=1)]
    reduce_sum x5 -> x0, other arithmetic: 5.38 us -> none  [the longest x1 2.39 us: build_kernel(): tgt_sq = jnp.sum(target_pc * target_pc, axis=0)]
    unnamed x12 -> x10, local copies, waits for them, and re-layouts: 1.66 us -> 5.87 us
  transfers between devices with their start and end apart: 3 -> 0, of which waited for: 3 -> 0; matrix products, arithmetic and copies ran while one was open for 4% -> 0% of each run, Pallas kernels for 0% -> 0%
where the time goes in v1:
time: 54.8 us; the launch traced here: 54.6 us
  Pallas kernels  48.7 us (89%)
  local copies, waits for them, and re-layouts  5.87 us (11%)
    pallas_call x1, Pallas kernels, fused_call(): pl.pallas_call(functools.partial(fused, n, components), out_shape=jax.Sha...  48.7 us
    unnamed x10, local copies, waits for them, and re-layouts  5.87 us

profile of v1, /device:TPU:0, one launch (start us, length us, event | category | flops | bytes accessed | tf_op | source)
XLA Modules:
  0.0 54.6 jit_solution(8608160608573954434)
XLA Ops:
  0.0 1.3 %copy.7.load_ref = bf16[2560,50]{1,0:T(8,128)(2,1)S(1)} copy(bf16[2560,50]{0,1:T(8,128)(2,1)} %param.8) | data formatting | bytes 512000 | tf_op args[2]
  1.3 0.0 copy-start
  1.3 1.7 %copy-done = bf16[2560,512]{1,0:T(8,128)(2,1)S(1)} copy-done((bf16[2560,512]{1,0:T(8,128)(2,1)S(1)}, bf16[2560,512]{1,0:T(8,128)(2,1)}, u32[]{:S(2)}) %copy-start) | copy-done | bytes 2621464
  3.0 0.0 copy-start.1
  3.1 0.7 %copy-done.1 = s32[4096]{0:T(1024)S(1)} copy-done((s32[4096]{0:T(1024)S(1)}, s32[4096]{0:T(1024)}, u32[]{:S(2)}) %copy-start.1) | copy-done | bytes 16408
  3.8 0.0 copy-start.2
  3.8 0.7 %copy-done.2 = s32[96]{0:T(128)S(1)} copy-done((s32[96]{0:T(128)S(1)}, s32[96]{0:T(128)}, u32[]{:S(2)}) %copy-start.2) | copy-done | bytes 408
  4.4 0.0 copy-start.3
  4.4 0.7 %copy-done.3 = s32[64]{0:T(128)S(1)} copy-done((s32[64]{0:T(128)S(1)}, s32[64]{0:T(128)}, u32[]{:S(2)}) %copy-start.3) | copy-done | bytes 280
  5.1 48.7 %shard_map.64 = f32[64,2048]{1,0:T(8,128)S(1)} custom-call(bf16[2560,512]{1,0:T(8,128)(2,1)S(1)} %copy-done, bf16[2560,4096]{1,0:T(8,128)(2,1)} %target_hbm.1, bf16[2560,50]{1,0:T(8,128)(2,1)S(1)} %copy.7.load_ref, s32[1,96]{1,0:T(1,128)S(1)} %bitcast.4, s32[1,64]{1,0:T(1,128)S(1)} %bitcast.5, s32[1,4096]{1,0:T(1,128)S(1)} %bitcast.3), custom_call_target="tpu_custom_call" | custom-call | tf_op jit(solution)/shard_map/pallas_call | solution.py:340
  53.8 0.8 %copy.9 = f32[64,2048]{1,0:T(8,128)} copy(f32[64,2048]{1,0:T(8,128)S(1)} %shard_map.64) | data formatting | bytes 1048576
Async XLA Ops:
  1.3 1.7 %copy-start = (bf16[2560,512]{1,0:T(8,128)(2,1)S(1)}, bf16[2560,512]{1,0:T(8,128)(2,1)}, u32[]{:S(2)}) copy-start(bf16[2560,512]{1,0:T(8,128)(2,1)} %source_hbm.1) | copy-start | bytes 7864324
  3.0 0.7 %copy-start.1 = (s32[4096]{0:T(1024)S(1)}, s32[4096]{0:T(1024)}, u32[]{:S(2)}) copy-start(s32[4096]{0:T(1024)} %param.11) | copy-start | bytes 49156
  3.8 0.7 %copy-start.2 = (s32[96]{0:T(128)S(1)}, s32[96]{0:T(128)}, u32[]{:S(2)}) copy-start(s32[96]{0:T(128)} %param.9) | copy-start | bytes 1156
  4.4 0.7 %copy-start.3 = (s32[64]{0:T(128)S(1)}, s32[64]{0:T(128)}, u32[]{:S(2)}) copy-start(s32[64]{0:T(128)} %param.10) | copy-start | bytes 772

commit v2 on v0

--- a/solution.py
+++ b/solution.py
@@ -1,6 +1,10 @@
+import functools
+
 import jax
 import jax.numpy as jnp
 from jax import lax
+from jax.experimental import pallas as pl
+from jax.experimental.pallas import tpu as pltpu
 from jax.sharding import PartitionSpec as P
 
 LEVELS = 4
@@ -72,10 +76,378 @@
         scale_v = (target_mass / lax.psum(col_part, "src")) ** power
     return jnp.float32(total_targets) * scale_u[:, None] * stored * scale_v[None, :]
 
+def proj(left, right):
+    return lax.dot_general(left, right, (((1,), (0,)), ((), ())), preferred_element_type=jnp.float32)
+
+
+def proj_nt(left, right, precision=None):
+    return lax.dot_general(
+        left, right, (((1,), (1,)), ((), ())), precision=precision, preferred_element_type=jnp.float32
+    )
+
+
+def power_of(x):
+    return jnp.exp(jnp.log(x) * (1.0 / 1.1))
+
+
+def iota(shape, axis):
+    return lax.broadcasted_iota(jnp.int32, shape, axis)
+
+
+def halves(x):
+    top = x.astype(jnp.bfloat16).astype(jnp.float32)
+    rest = x - top
+    middle = rest.astype(jnp.bfloat16).astype(jnp.float32)
+    return top, middle, rest - middle
+
+
+def replicate(row):
+    return jnp.transpose(jnp.broadcast_to(row, (128, row.shape[1])))
+
+
+def fused(
+    n, source_hbm, target_hbm, load_ref, panel_hbm, label_hbm, order_hbm, out_ref,
+    panel_ref, label_ref, order_ref,
+    xs, xt, weights, part_t, recv_x, sum_t, recv_t, part_s, recv_s, all_t, all_s, rows, lookup, perm, moments,
+    kern, row_u, col_v,
+    load_sem, small_sem, rx_send, rx_recv, rt_send, rt_recv, rs_send, rs_recv, as_send, as_recv, fs_send, fs_recv,
+    ax_send, ax_recv, az_send, az_recv, fw_send, fw_recv, it_send, it_recv,
+):
+    me = lax.axis_index("src")
+    core = lax.axis_index("tgt")
+    nz = n // 2
+    x = lax.rem(me, 2)
+    z = me // 2
+    beside = 2 * z + 1 - x
+    components, genes = load_ref.shape
+    width = xt.shape[2]
+    half_s = xs.shape[1]
+    high = part_t.shape[1]
+    n_targets = target_hbm.shape[1]
+    n_sources = source_hbm.shape[1]
+    own = out_ref.shape[0]
+    columns = out_ref.shape[1]
+    deep = 8 * n
+
+    def peer(d):
+        return lax.rem(me + d, n)
+
+    def along(d):
+        return lax.rem(z + d, nz)
+
+    def remote(src, dst, send, recv, s, c):
+        return pltpu.make_async_remote_copy(
+            src_ref=src, dst_ref=dst, send_sem=send, recv_sem=recv,
+            device_id={"src": s, "tgt": c}, device_id_type=pl.DeviceIdType.MESH,
+        )
+
+    sends = []
+
+    def go(copy):
+        copy.start()
+        sends.append(copy)
+
+    turn = [n // 2 + k * sign for k in range(n // 2) for sign in ((1, -1) if k else (1,))]
+    line = [nz // 2] + [d for d in range(1, nz) if d != nz // 2] + [0]
+
+    barrier = pltpu.get_barrier_semaphore()
+    for d in range(1, n):
+        pl.semaphore_signal(
+            barrier, inc=1, device_id={"src": peer(d), "tgt": core}, device_id_type=pl.DeviceIdType.MESH
+        )
+    pl.semaphore_signal(
+        barrier, inc=1, device_id={"src": me, "tgt": 1 - core}, device_id_type=pl.DeviceIdType.MESH
+    )
+
+    small = []
+    my_columns = pl.multiple_of(core * columns, 128)
+    for k, (src, dst) in enumerate((
+        (panel_hbm, panel_ref), (label_hbm, label_ref),
+        (order_hbm.at[:, pl.ds(my_columns, columns)], order_ref),
+    )):
+        small.append(pltpu.make_async_copy(src, dst, small_sem.at[k]))
+        small[-1].start()
+    load_s = pltpu.make_async_copy(
+        source_hbm.at[:, pl.ds(pl.multiple_of(core * half_s, 128), half_s)], xs, load_sem.at[n]
+    )
+    load_s.start()
+    plan = [(d, 2 * along(d) + 1 - x) for d in line] + [(d, 2 * along(d) + x) for d in line]
+    loads = []
+    for k, (d, s) in enumerate(plan):
+        start = pl.multiple_of(core * columns + s * width, 128)
+        load = pltpu.make_async_copy(target_hbm.at[:, pl.ds(start, width)], xt.at[k], load_sem.at[k])
+        load.start()
+        loads.append(load)
+
+    for copy in small:
+        copy.wait()
+    base = jnp.concatenate(
+        [load_ref[...].astype(jnp.float32), jnp.zeros((deep - components, genes), jnp.float32)], axis=0
+    )
+    hits = (iota((genes, panel_ref.shape[1]), 0) + me * genes == panel_ref[...]).astype(jnp.float32)
+    pick = (iota((deep, panel_ref.shape[1]), 0) == components).astype(jnp.bfloat16)
+    counts = proj_nt(pick, hits.astype(jnp.bfloat16))
+    weights[0] = base.astype(jnp.bfloat16)
+    weights[1] = (base + counts).astype(jnp.bfloat16)
+
+    spans = 0.5 * (LEVELS - label_ref[...].astype(jnp.float32))
+    place = (iota((own, half_s), 0) + me * own == iota((own, half_s), 1) + core * half_s).astype(jnp.bfloat16)
+    placed = proj(jnp.broadcast_to(spans, (16, own)).astype(jnp.bfloat16), place)[0:1]
+    load_s.wait()
+    source_part = proj(weights[1], xs[...])
+    part_s[...] = jnp.where(iota((deep, half_s), 0) == components + 1, placed, source_part)
+    recv_s[me] = part_s[pl.ds(pl.multiple_of(me * 8, 8), 8), :]
+
+    pl.semaphore_wait(barrier, n)
+    for d in turn:
+        p = peer(d)
+        go(remote(part_s.at[pl.ds(pl.multiple_of(p * 8, 8), 8)], recv_s.at[me], rs_send.at[d], rs_recv.at[me], p, core))
+
+    for k, (d, s) in enumerate(plan):
+        loads[k].wait()
+        block = proj(weights[0], xt[k])[:high]
+        zz = along(d)
+        if k < nz:
+            part_t[k] = block
+            go(remote(part_t.at[k], recv_x.at[zz], rx_send.at[k], rx_recv.at[zz], beside, core))
+        else:
+            remote(recv_x.at[zz], recv_x.at[zz], rx_send.at[k - nz], rx_recv.at[zz], beside, core).wait_recv()
+            block = block + recv_x[zz]
+            if d:
+                sum_t[d] = block
+                go(remote(sum_t.at[d], recv_t.at[z], rt_send.at[d], rt_recv.at[z], s, core))
+            else:
+                recv_t[z] = block
+
+    for d in turn:
+        p = peer(d)
+        remote(recv_s.at[p], recv_s.at[p], rs_send.at[d], rs_recv.at[p], p, core).wait_recv()
+    my_lanes = pl.ds(pl.multiple_of(core * half_s, 128), half_s)
+    other_lanes = pl.ds(pl.multiple_of((1 - core) * half_s, 128), half_s)
+
+    def rows_of(s):
+        return pl.ds(pl.multiple_of(s * 8, 8), 8)
+
+    total = recv_s[0]
+    for s in range(1, n):
+        total = total + recv_s[s]
+    all_s[rows_of(me), my_lanes] = total
+    here = all_s.at[rows_of(me), my_lanes]
+    for d in turn:
+        go(remote(here, here, as_send.at[d], as_recv.at[me], peer(d), core))
+    go(remote(here, here, fs_send.at[0], fs_recv.at[me], me, 1 - core))
+
+    order = order_ref[...]
+    block_of = order // width
+    lookup[...] = (iota((width, columns), 0) == order - block_of * width).astype(jnp.float32).astype(jnp.bfloat16)
+    perm[...] = jnp.zeros_like(perm)
+    moments[...] = jnp.zeros_like(moments)
+
+    def place_block(index):
+        block = all_t[index]
+        moments[0] += block
+        moments[1] += block * block
+        found = proj(jnp.concatenate(halves(block), axis=0).astype(jnp.bfloat16), lookup[...])
+        found = (found[:high] + found[high : 2 * high]) + found[2 * high :]
+        perm[:high] = jnp.where(block_of == index, found, perm[:high])
+
+    for d in line[:-1]:
+        zz = along(d)
+        remote(recv_t.at[zz], recv_t.at[zz], rt_send.at[d], rt_recv.at[zz], 2 * zz + x, core).wait_recv()
+    mine = recv_t[0]
+    for s in range(1, nz):
+        mine = mine + recv_t[s]
+    slot = core * n + me
+    all_t[slot] = mine
+    here = all_t.at[slot]
+    for d in line[:-1]:
+        go(remote(here, here, az_send.at[d], az_recv.at[z], 2 * along(d) + x, core))
+    go(remote(here, here, ax_send.at[0], ax_recv.at[z], beside, core))
+    go(remote(here, here, fw_send.at[0, 0], fw_recv.at[me], me, 1 - core))
+
+    for d in turn:
+        p = peer(d)
+        there = all_s.at[rows_of(p), my_lanes]
+        remote(there, there, as_send.at[d], as_recv.at[p], p, core).wait_recv()
+        go(remote(there, there, fs_send.at[d], fs_recv.at[p], me, 1 - core))
+    place_block(slot)
+    for d in line[:-1][::-1]:
+        zz = along(d)
+        s = 2 * zz + x
+        there = all_t.at[core * n + s]
+        remote(there, there, az_send.at[d], az_recv.at[zz], s, core).wait_recv()
+        go(remote(there, there, ax_send.at[d], ax_recv.at[zz], beside, core))
+        go(remote(there, there, fw_send.at[0, d], fw_recv.at[s], me, 1 - core))
+        place_block(core * n + s)
+    for d in line[::-1]:
+        zz = along(d)
+        s = 2 * zz + 1 - x
+        there = all_t.at[core * n + s]
+        remote(there, there, ax_send.at[d], ax_recv.at[zz], beside, core).wait_recv()
+        go(remote(there, there, fw_send.at[1, d], fw_recv.at[s], me, 1 - core))
+        place_block(core * n + s)
+
+    for d in range(n):
+        p = peer(d)
+        there = all_s.at[rows_of(p), other_lanes]
+        remote(there, there, fs_send.at[d], fs_recv.at[p], me, 1 - core).wait_recv()
+    source = all_s[...]
+    growth = jnp.exp(
+        source[components + 1 : components + 2]
+        * jnp.clip(source[components : components + 1] / jnp.sqrt(jnp.float32(panel_ref.shape[1])), -2.0, 2.0)
+    )
+    pcs = jnp.where(iota(source.shape, 0) < components, source, 0.0)
+    source_sq = jnp.sum(pcs * pcs, axis=0, keepdims=True)
+    source_rep = replicate(source_sq)
+    turned = jnp.transpose(jnp.concatenate([pcs, jnp.zeros((128 - deep, n_sources), jnp.float32)], axis=0))
+    s_top, s_mid, s_low = halves(turned[:, :deep])
+    left = jnp.concatenate([s_top, s_mid, s_top, s_mid, s_low, s_top], axis=1).astype(jnp.bfloat16)
+
+    for d in range(n):
+        p = peer(d)
+        there = all_t.at[(1 - core) * n + p]
+        remote(there, there, fw_send.at[0, 0], fw_recv.at[p], me, 1 - core).wait_recv()
+
+    @pl.loop(0, n)
+    def _(k):
+        place_block((1 - core) * n + k)
+
+    target_sum = jnp.sum(moments[0], axis=1, keepdims=True)
+    target_sq = jnp.sum(jnp.sum(moments[1], axis=1, keepdims=True), axis=0, keepdims=True)
+    source_sum = jnp.sum(pcs[:high], axis=1, keepdims=True)
+    mean = (
+        jnp.sum(source_sq, axis=1, keepdims=True) / n_sources
+        + target_sq / n_targets
+        - 2.0 * jnp.sum((source_sum / n_sources) * (target_sum / n_targets), axis=0, keepdims=True)
+    )
+    factor = -1.0 / (0.1 * mean)
+    tiles = columns // 128
+
+    def lanes(t):
+        return slice(t * 128, t * 128 + 128)
+
+    step_rows = 64
+
+    for t in range(0, tiles, 2):
+        wide = slice(t * 128, t * 128 + 256)
+        part = perm[:, wide]
+        norm = jnp.sum(part * part, axis=0, keepdims=True)
+        t_top, t_mid, t_low = halves(part)
+        right = jnp.concatenate([t_top, t_top, t_mid, t_mid, t_top, t_low], axis=0).astype(jnp.bfloat16)
+        cross = proj(left, right)
+        for h in range(2):
+            d2 = source_rep + norm[:, lanes(h)] - 2.0 * cross[:, lanes(h)]
+            kern[:, lanes(t + h)] = jnp.exp(d2 * factor)
+
+    def row_sums(scale):
+        out = []
+        for r in range(0, n_sources, step_rows):
+            acc = None
+            for t in range(tiles):
+                term = kern[r : r + step_rows, lanes(t)]
+                if scale:
+                    term = term * col_v[:, lanes(t)]
+                acc = term if acc is None else acc + term
+            out.append(acc)
+        return jnp.sum(jnp.transpose(jnp.concatenate(out, axis=0)), axis=0, keepdims=True)
+
+    target_mass = n_sources / n_targets
+    for step in range(ITERS):
+        rows[step, core] = row_sums(step > 0)
+        here = rows.at[step, core]
+        go(remote(here, here, it_send.at[step], it_recv.at[step], me, 1 - core))
+        there = rows.at[step, 1 - core]
+        remote(there, there, it_send.at[step], it_recv.at[step], me, 1 - core).wait_recv()
+        row_u[...] = replicate(power_of(growth / (rows[step, 0] + rows[step, 1])))
+        for t in range(tiles):
+            col_v[:, lanes(t)] = jnp.sum(kern[:, lanes(t)] * row_u[...], axis=0, keepdims=True)
+        col_v[...] = power_of(target_mass / col_v[...])
+    mine_rows = pl.ds(pl.multiple_of(me * own, 8), own)
+    own_u = n_targets * row_u[mine_rows, :]
+    for t in range(tiles):
+        out_ref[:, lanes(t)] = own_u * kern[mine_rows, lanes(t)] * col_v[:, lanes(t)]
+    for copy in sends:
+        copy.wait_send()
+
+
+def fused_call(source_expr, target_expr, loadings, panel, time_label, target_order):
+    n = lax.axis_size("src")
+    genes, components = loadings.shape
+    n_sources, n_targets = source_expr.shape[1], target_expr.shape[1]
+    own, columns = n_sources // n, n_targets // 2
+    width, half_s = columns // n, n_sources // 2
+    high = (components + 7) // 8 * 8
+    nz = n // 2
+    vmem = pltpu.VMEM
+    dma = pltpu.SemaphoreType.DMA
+    f32, bf16, i32 = jnp.float32, jnp.bfloat16, jnp.int32
+    return pl.pallas_call(
+        functools.partial(fused, n),
+        out_shape=jax.ShapeDtypeStruct((own, columns), f32),
+        in_specs=[pl.BlockSpec(memory_space=vmem if k == 2 else pltpu.HBM) for k in range(6)],
+        out_specs=pl.BlockSpec(memory_space=vmem),
+        scratch_shapes=[
+            vmem((1, panel.shape[0]), i32),
+            vmem((1, own), i32),
+            vmem((1, columns), i32),
+            vmem((genes, half_s), bf16),
+            vmem((n, genes, width), bf16),
+            vmem((2, 8 * n, genes), bf16),
+            vmem((nz, high, width), f32),
+            vmem((nz, high, width), f32),
+            vmem((nz, high, width), f32),
+            vmem((nz, high, width), f32),
+            vmem((8 * n, half_s), f32),
+            vmem((n, 8, half_s), f32),
+            vmem((2 * n, high, width), f32),
+            vmem((8 * n, n_sources), f32),
+            vmem((ITERS, 2, 1, n_sources), f32),
+            vmem((width, columns), bf16),
+            vmem((8 * n, columns), f32),
+            vmem((2, high, width), f32),
+            vmem((n_sources, columns), f32),
+            vmem((n_sources, 128), f32),
+            vmem((1, columns), f32),
+            dma((n + 1,)), dma((3,)),
+            dma((nz,)), dma((nz,)), dma((nz,)), dma((nz,)),
+            dma((n,)), dma((n,)), dma((n,)), dma((n,)), dma((n,)), dma((n,)),
+            dma((nz,)), dma((nz,)), dma((nz,)), dma((nz,)),
+            dma((2, nz)), dma((n,)), dma((ITERS,)), dma((ITERS,)),
+        ],
+        compiler_params=pltpu.CompilerParams(
+            collective_id=0, has_side_effects=True, vmem_limit_bytes=48 * 1024 * 1024
+        ),
+    )(
+        source_expr, target_expr, loadings.T,
+        panel.reshape(1, -1), time_label.reshape(1, -1), target_order.reshape(1, -1),
+    )
+
+
+def fits(mesh, source_expr, target_expr, loadings, time_label):
+    n = mesh.shape["src"]
+    components = loadings.shape[1]
+    n_sources, n_targets = source_expr.shape[1], target_expr.shape[1]
+    return (
+        mesh.shape["tgt"] == 2
+        and n % 2 == 0
+        and components + 2 <= 8 * n
+        and 8 * n <= 128
+        and n_sources % 256 == 0
+        and n_sources * n_targets <= 2 * 1024 * 1024
+        and n_targets % (2 * n * 128) == 0
+        and loadings.shape[0] % 128 == 0
+        and loadings.shape[0] * (n_targets + n_sources) <= 32 * 1024 * 1024
+    )
+
 
 def solution(mesh):
+    def per_device(*arrays):
+        if fits(mesh, arrays[0], arrays[1], arrays[2], arrays[4]):
+            return fused_call(*arrays)
+        return local(*arrays)
+
     return jax.shard_map(
-        local,
+        per_device,
         mesh=mesh,
         in_specs=(
             P("src", "pairs"),

time: 341 us -> 43.6 us (0.13)
  waiting for transfers between devices: 192 us -> 0 us
  blocking collectives: 92.1 us -> 0 us
  Pallas kernels: 0 us -> 37.8 us
  matrix products: 18.8 us -> 0 us
  between operations: 16.4 us -> 0.01 us
  local copies, waits for them, and re-layouts: 14 us -> 5.52 us
  other arithmetic: 7.15 us -> 0 us
    unnamed x5 -> x0, waiting for transfers between devices: 116 us -> none
    psum x7 -> x0, blocking collectives: 92.1 us -> none  [the longest x3 54.2 us: local(): scale_v = (target_mass / lax.psum(col_part, 'src')) ** power]
    psum x1 -> x0, waiting for transfers between devices: 76.1 us -> none  [local(): target_all = lax.psum(gene_sum(loadings, target_expr), 'src')]
    pallas_call x0 -> x1, Pallas kernels: none -> 37.8 us  [fused_call(): pl.pallas_call(functools.partial(fused, n), out_shape=jax.ShapeDtypeStruc...]
    dot_general x8 -> x0, matrix products: 15.2 us -> none  [the longest x1 9.79 us: gene_sum(): lax.dot_general(left, right, (((0,), (0,)), ((), ())), preferred_element_...]
    gather x1 -> x0, local copies, waits for them, and re-layouts: 9.15 us -> none  [local(): target_pc = jnp.take(target_all, local_order, axis=1)]
    reduce_sum x5 -> x0, other arithmetic: 5.38 us -> none  [the longest x1 2.39 us: build_kernel(): tgt_sq = jnp.sum(target_pc * target_pc, axis=0)]
    unnamed x12 -> x11, local copies, waits for them, and re-layouts: 1.66 us -> 5.52 us
  transfers between devices with their start and end apart: 3 -> 0, of which waited for: 3 -> 0; matrix products, arithmetic and copies ran while one was open for 4% -> 0% of each run, Pallas kernels for 0% -> 0%
where the time goes in v2:
time: 43.6 us; the launch traced here: 43.4 us
  Pallas kernels  37.8 us (87%)
  local copies, waits for them, and re-layouts  5.52 us (13%)
    pallas_call x1, Pallas kernels, fused_call(): pl.pallas_call(functools.partial(fused, n), out_shape=jax.ShapeDtypeStruc...  37.8 us
    unnamed x11, local copies, waits for them, and re-layouts  5.52 us

profile of v2, /device:TPU:0, one launch (start us, length us, event | category | flops | bytes accessed | tf_op | source)
XLA Modules:
  0.0 43.4 jit_solution(7807018779824489)
XLA Ops:
  0.0 0.0 copy-start
  0.0 1.7 %copy-done = bf16[2560,512]{1,0:T(8,128)(2,1)S(1)} copy-done((bf16[2560,512]{1,0:T(8,128)(2,1)S(1)}, bf16[2560,512]{1,0:T(8,128)(2,1)}, u32[]{:S(2)}) %copy-start) | copy-done | bytes 2621464
  1.7 0.0 copy-start.1
  1.7 1.0 %copy-done.1 = bf16[2560,50]{0,1:T(8,128)(2,1)S(1)} copy-done((bf16[2560,50]{0,1:T(8,128)(2,1)S(1)}, bf16[2560,50]{0,1:T(8,128)(2,1)}, u32[]{:S(2)}) %copy-start.1) | copy-done | bytes 256024
  2.7 0.0 copy-start.2
  2.7 0.7 %copy-done.2 = s32[4096]{0:T(1024)S(1)} copy-done((s32[4096]{0:T(1024)S(1)}, s32[4096]{0:T(1024)}, u32[]{:S(2)}) %copy-start.2) | copy-done | bytes 16408
  3.4 0.0 copy-start.3
  3.4 0.7 %copy-done.3 = s32[96]{0:T(128)S(1)} copy-done((s32[96]{0:T(128)S(1)}, s32[96]{0:T(128)}, u32[]{:S(2)}) %copy-start.3) | copy-done | bytes 408
  4.1 0.0 copy-start.4
  4.1 0.7 %copy-done.4 = s32[64]{0:T(128)S(1)} copy-done((s32[64]{0:T(128)S(1)}, s32[64]{0:T(128)}, u32[]{:S(2)}) %copy-start.4) | copy-done | bytes 280
  4.7 37.8 %shard_map.64 = f32[64,2048]{1,0:T(8,128)S(1)} custom-call(bf16[2560,512]{1,0:T(8,128)(2,1)S(1)} %copy-done, bf16[2560,4096]{1,0:T(8,128)(2,1)} %target_hbm.1, bf16[50,2560]{1,0:T(8,128)(2,1)S(1)} %bitcast.4, s32[1,96]{1,0:T(1,128)S(1)} %bitcast.6, s32[1,64]{1,0:T(1,128)S(1)} %bitcast.7, s32[1,4096]{1,0:T(1,128)S(1)} %bitcast.5), custom_call_target="tpu_custom_call" | custom-call | tf_op jit(solution)/shard_map/pallas_call | solution.py:384
  42.6 0.8 %copy.8 = f32[64,2048]{1,0:T(8,128)} copy(f32[64,2048]{1,0:T(8,128)S(1)} %shard_map.64) | data formatting | bytes 1048576
Async XLA Ops:
  0.0 1.7 %copy-start = (bf16[2560,512]{1,0:T(8,128)(2,1)S(1)}, bf16[2560,512]{1,0:T(8,128)(2,1)}, u32[]{:S(2)}) copy-start(bf16[2560,512]{1,0:T(8,128)(2,1)} %source_hbm.1) | copy-start | bytes 7864324
  1.7 1.0 %copy-start.1 = (bf16[2560,50]{0,1:T(8,128)(2,1)S(1)}, bf16[2560,50]{0,1:T(8,128)(2,1)}, u32[]{:S(2)}) copy-start(bf16[2560,50]{0,1:T(8,128)(2,1)} %param.8) | copy-start | bytes 768004
  2.7 0.7 %copy-start.2 = (s32[4096]{0:T(1024)S(1)}, s32[4096]{0:T(1024)}, u32[]{:S(2)}) copy-start(s32[4096]{0:T(1024)} %param.11) | copy-start | bytes 49156
  3.4 0.7 %copy-start.3 = (s32[96]{0:T(128)S(1)}, s32[96]{0:T(128)}, u32[]{:S(2)}) copy-start(s32[96]{0:T(128)} %param.9) | copy-start | bytes 1156
  4.1 0.7 %copy-start.4 = (s32[64]{0:T(128)S(1)}, s32[64]{0:T(128)}, u32[]{:S(2)}) copy-start(s32[64]{0:T(128)} %param.10) | copy-start | bytes 772

commit v3 on v2

--- a/solution.py
+++ b/solution.py
@@ -167,29 +167,41 @@
     )):
         small.append(pltpu.make_async_copy(src, dst, small_sem.at[k]))
         small[-1].start()
+    plan = [(d, 2 * along(d) + 1 - x) for d in line] + [(d, 2 * along(d) + x) for d in line]
     load_s = pltpu.make_async_copy(
         source_hbm.at[:, pl.ds(pl.multiple_of(core * half_s, 128), half_s)], xs, load_sem.at[n]
     )
-    load_s.start()
-    plan = [(d, 2 * along(d) + 1 - x) for d in line] + [(d, 2 * along(d) + x) for d in line]
     loads = []
     for k, (d, s) in enumerate(plan):
+        if k == nz:
+            load_s.start()
         start = pl.multiple_of(core * columns + s * width, 128)
         load = pltpu.make_async_copy(target_hbm.at[:, pl.ds(start, width)], xt.at[k], load_sem.at[k])
         load.start()
         loads.append(load)
 
+    base = jnp.concatenate(
+        [load_ref[...].astype(jnp.float32), jnp.zeros((deep - components, genes), jnp.float32)], axis=0
+    )
+    weights[0] = base.astype(jnp.bfloat16)
+
+    def project(k):
+        loads[k].wait()
+        return proj(weights[0], xt[k])[:high]
+
+    for k in range(nz):
+        zz = along(plan[k][0])
+        part_t[k] = project(k)
+        if k == 0:
+            pl.semaphore_wait(barrier, n)
+        go(remote(part_t.at[k], recv_x.at[zz], rx_send.at[k], rx_recv.at[zz], beside, core))
+
     for copy in small:
         copy.wait()
-    base = jnp.concatenate(
-        [load_ref[...].astype(jnp.float32), jnp.zeros((deep - components, genes), jnp.float32)], axis=0
-    )
     hits = (iota((genes, panel_ref.shape[1]), 0) + me * genes == panel_ref[...]).astype(jnp.float32)
     pick = (iota((deep, panel_ref.shape[1]), 0) == components).astype(jnp.bfloat16)
     counts = proj_nt(pick, hits.astype(jnp.bfloat16))
-    weights[0] = base.astype(jnp.bfloat16)
-    weights[1] = (base + counts).astype(jnp.bfloat16)
-
+    weights[1] = (weights[0].astype(jnp.float32) + counts).astype(jnp.bfloat16)
     spans = 0.5 * (LEVELS - label_ref[...].astype(jnp.float32))
     place = (iota((own, half_s), 0) + me * own == iota((own, half_s), 1) + core * half_s).astype(jnp.bfloat16)
     placed = proj(jnp.broadcast_to(spans, (16, own)).astype(jnp.bfloat16), place)[0:1]
@@ -197,27 +209,21 @@
     source_part = proj(weights[1], xs[...])
     part_s[...] = jnp.where(iota((deep, half_s), 0) == components + 1, placed, source_part)
     recv_s[me] = part_s[pl.ds(pl.multiple_of(me * 8, 8), 8), :]
-
-    pl.semaphore_wait(barrier, n)
     for d in turn:
         p = peer(d)
         go(remote(part_s.at[pl.ds(pl.multiple_of(p * 8, 8), 8)], recv_s.at[me], rs_send.at[d], rs_recv.at[me], p, core))
 
-    for k, (d, s) in enumerate(plan):
-        loads[k].wait()
-        block = proj(weights[0], xt[k])[:high]
+    for k in range(nz, n):
+        d, s = plan[k]
         zz = along(d)
-        if k < nz:
-            part_t[k] = block
-            go(remote(part_t.at[k], recv_x.at[zz], rx_send.at[k], rx_recv.at[zz], beside, core))
+        block = project(k)
+        remote(recv_x.at[zz], recv_x.at[zz], rx_send.at[k - nz], rx_recv.at[zz], beside, core).wait_recv()
+        block = block + recv_x[zz]
+        if d:
+            sum_t[d] = block
+            go(remote(sum_t.at[d], recv_t.at[z], rt_send.at[d], rt_recv.at[z], s, core))
         else:
-            remote(recv_x.at[zz], recv_x.at[zz], rx_send.at[k - nz], rx_recv.at[zz], beside, core).wait_recv()
-            block = block + recv_x[zz]
-            if d:
-                sum_t[d] = block
-                go(remote(sum_t.at[d], recv_t.at[z], rt_send.at[d], rt_recv.at[z], s, core))
-            else:
-                recv_t[z] = block
+            recv_t[z] = block
 
     for d in turn:
         p = peer(d)
@@ -243,13 +249,17 @@
     perm[...] = jnp.zeros_like(perm)
     moments[...] = jnp.zeros_like(moments)
 
-    def place_block(index):
-        block = all_t[index]
-        moments[0] += block
-        moments[1] += block * block
-        found = proj(jnp.concatenate(halves(block), axis=0).astype(jnp.bfloat16), lookup[...])
-        found = (found[:high] + found[high : 2 * high]) + found[2 * high :]
-        perm[:high] = jnp.where(block_of == index, found, perm[:high])
+    def place_pair(first, second):
+        parts = []
+        for index in (first, second):
+            block = all_t[index]
+            moments[0] += block
+            moments[1] += block * block
+            parts += halves(block)
+        found = proj(jnp.concatenate(parts, axis=0).astype(jnp.bfloat16), lookup[...])
+        one = (found[:high] + found[high : 2 * high]) + found[2 * high : 3 * high]
+        two = (found[3 * high : 4 * high] + found[4 * high : 5 * high]) + found[5 * high :]
+        perm[:high] = jnp.where(block_of == first, one, jnp.where(block_of == second, two, perm[:high]))
 
     for d in line[:-1]:
         zz = along(d)
@@ -263,29 +273,50 @@
     for d in line[:-1]:
         go(remote(here, here, az_send.at[d], az_recv.at[z], 2 * along(d) + x, core))
     go(remote(here, here, ax_send.at[0], ax_recv.at[z], beside, core))
-    go(remote(here, here, fw_send.at[0, 0], fw_recv.at[me], me, 1 - core))
+    go(remote(here, here, fw_send.at[0], fw_recv.at[me], me, 1 - core))
 
     for d in turn:
         p = peer(d)
         there = all_s.at[rows_of(p), my_lanes]
         remote(there, there, as_send.at[d], as_recv.at[p], p, core).wait_recv()
         go(remote(there, there, fs_send.at[d], fs_recv.at[p], me, 1 - core))
-    place_block(slot)
-    for d in line[:-1][::-1]:
-        zz = along(d)
-        s = 2 * zz + x
+
+    def nth(k):
+        across = k // nz
+        zz = lax.rem(z + k, nz)
+        return zz, 2 * zz + x + across * (1 - 2 * x)
+
+    def by_line(k):
+        zz, s = nth(k)
         there = all_t.at[core * n + s]
-        remote(there, there, az_send.at[d], az_recv.at[zz], s, core).wait_recv()
-        go(remote(there, there, ax_send.at[d], ax_recv.at[zz], beside, core))
-        go(remote(there, there, fw_send.at[0, d], fw_recv.at[s], me, 1 - core))
-        place_block(core * n + s)
-    for d in line[::-1]:
-        zz = along(d)
-        s = 2 * zz + 1 - x
+        return remote(there, there, az_send.at[k], az_recv.at[zz], s, core)
+
+    def by_x(k):
+        zz, s = nth(k)
         there = all_t.at[core * n + s]
-        remote(there, there, ax_send.at[d], ax_recv.at[zz], beside, core).wait_recv()
-        go(remote(there, there, fw_send.at[1, d], fw_recv.at[s], me, 1 - core))
-        place_block(core * n + s)
+        return remote(there, there, ax_send.at[lax.rem(k, nz)], ax_recv.at[zz], beside, core)
+
+    def by_core(k, c):
+        zz, s = nth(k)
+        there = all_t.at[c * n + s]
+        return remote(there, there, fw_send.at[k], fw_recv.at[s], me, 1 - core)
+
+    @pl.loop(1, n + 1)
+    def _(k):
+        @pl.when(k < nz)
+        def _():
+            by_line(k).wait_recv()
+            by_x(k).start()
+            by_core(k, core).start()
+
+        @pl.when((k >= nz) & (k < n))
+        def _():
+            by_x(k).wait_recv()
+            by_core(k, core).start()
+
+        by_core(k - 1, 1 - core).wait_recv()
+        zz, s = nth(k - 1)
+        place_pair(core * n + s, (1 - core) * n + s)
 
     for d in range(n):
         p = peer(d)
@@ -303,15 +334,6 @@
     s_top, s_mid, s_low = halves(turned[:, :deep])
     left = jnp.concatenate([s_top, s_mid, s_top, s_mid, s_low, s_top], axis=1).astype(jnp.bfloat16)
 
-    for d in range(n):
-        p = peer(d)
-        there = all_t.at[(1 - core) * n + p]
-        remote(there, there, fw_send.at[0, 0], fw_recv.at[p], me, 1 - core).wait_recv()
-
-    @pl.loop(0, n)
-    def _(k):
-        place_block((1 - core) * n + k)
-
     target_sum = jnp.sum(moments[0], axis=1, keepdims=True)
     target_sq = jnp.sum(jnp.sum(moments[1], axis=1, keepdims=True), axis=0, keepdims=True)
     source_sum = jnp.sum(pcs[:high], axis=1, keepdims=True)
@@ -328,16 +350,16 @@
 
     step_rows = 64
 
-    for t in range(0, tiles, 2):
-        wide = slice(t * 128, t * 128 + 256)
-        part = perm[:, wide]
+    @pl.loop(0, tiles // 2)
+    def _(t):
+        part = perm[:, pl.ds(pl.multiple_of(t * 256, 256), 256)]
         norm = jnp.sum(part * part, axis=0, keepdims=True)
         t_top, t_mid, t_low = halves(part)
         right = jnp.concatenate([t_top, t_top, t_mid, t_mid, t_top, t_low], axis=0).astype(jnp.bfloat16)
         cross = proj(left, right)
         for h in range(2):
             d2 = source_rep + norm[:, lanes(h)] - 2.0 * cross[:, lanes(h)]
-            kern[:, lanes(t + h)] = jnp.exp(d2 * factor)
+            kern[:, pl.ds(pl.multiple_of(t * 256 + h * 128, 128), 128)] = jnp.exp(d2 * factor)
 
     def row_sums(scale):
         out = []
@@ -368,6 +390,10 @@
         out_ref[:, lanes(t)] = own_u * kern[mine_rows, lanes(t)] * col_v[:, lanes(t)]
     for copy in sends:
         copy.wait_send()
+    for k in range(1, n):
+        if k < nz:
+            by_x(k).wait_send()
+        by_core(k, core).wait_send()
 
 
 def fused_call(source_expr, target_expr, loadings, panel, time_label, target_order):
@@ -412,10 +438,10 @@
             dma((nz,)), dma((nz,)), dma((nz,)), dma((nz,)),
             dma((n,)), dma((n,)), dma((n,)), dma((n,)), dma((n,)), dma((n,)),
             dma((nz,)), dma((nz,)), dma((nz,)), dma((nz,)),
-            dma((2, nz)), dma((n,)), dma((ITERS,)), dma((ITERS,)),
+            dma((n,)), dma((n,)), dma((ITERS,)), dma((ITERS,)),
         ],
         compiler_params=pltpu.CompilerParams(
-            collective_id=0, has_side_effects=True, vmem_limit_bytes=48 * 1024 * 1024
+            collective_id=0, has_side_effects=True, vmem_limit_bytes=56 * 1024 * 1024
         ),
     )(
         source_expr, target_expr, loadings.T,

time: 43.6 us -> 42.3 us (0.970)
  local copies, waits for them, and re-layouts: 5.52 us -> 1.87 us
  Pallas kernels: 37.8 us -> 40.2 us
    unnamed x11 -> x1, local copies, waits for them, and re-layouts: 5.52 us -> 1.87 us
    pallas_call x1, Pallas kernels: 37.8 us -> 40.2 us  [fused_call(): pl.pallas_call(functools.partial(fused, n), out_shape=jax.ShapeDtypeStruc...]
where the time goes in v3:
time: 42.3 us; the launch traced here: 42.1 us
  Pallas kernels  40.2 us (95%)
  local copies, waits for them, and re-layouts  1.87 us (4%)
    pallas_call x1, Pallas kernels, fused_call(): pl.pallas_call(functools.partial(fused, n), out_shape=jax.ShapeDtypeStruc...  40.2 us
    unnamed x1, local copies, waits for them, and re-layouts  1.87 us

profile of v3, /device:TPU:0, one launch (start us, length us, event | category | flops | bytes accessed | tf_op | source)
XLA Modules:
  0.0 42.1 jit_solution(13888532839503279644)
XLA Ops:
  0.0 40.2 %shard_map.64 = f32[64,2048]{1,0:T(8,128)} custom-call(bf16[2560,512]{1,0:T(8,128)(2,1)} %source_hbm.1, bf16[2560,4096]{1,0:T(8,128)(2,1)} %target_hbm.1, bf16[50,2560]{1,0:T(8,128)(2,1)} %bitcast.4, s32[1,96]{1,0:T(1,128)} %bitcast.6, s32[1,64]{1,0:T(1,128)} %bitcast.7, s32[1,4096]{1,0:T(1,128)} %bitcast.5), custom_call_target="tpu_custom_call" | custom-call | tf_op jit(solution)/shard_map/pallas_call | solution.py:410
  40.2 1.9 %copy.8 = f32[64,2048]{1,0:T(8,128)} copy(f32[64,2048]{1,0:T(8,128)} %shard_map.64) | data formatting | bytes 1048576

commit v4 on v3

--- a/solution.py
+++ b/solution.py
@@ -148,7 +148,7 @@
         sends.append(copy)
 
     turn = [n // 2 + k * sign for k in range(n // 2) for sign in ((1, -1) if k else (1,))]
-    line = [nz // 2] + [d for d in range(1, nz) if d != nz // 2] + [0]
+    line = list(range(nz))[::-1]
 
     barrier = pltpu.get_barrier_semaphore()
     for d in range(1, n):
@@ -171,14 +171,12 @@
     load_s = pltpu.make_async_copy(
         source_hbm.at[:, pl.ds(pl.multiple_of(core * half_s, 128), half_s)], xs, load_sem.at[n]
     )
-    loads = []
     for k, (d, s) in enumerate(plan):
         if k == nz:
             load_s.start()
         start = pl.multiple_of(core * columns + s * width, 128)
         load = pltpu.make_async_copy(target_hbm.at[:, pl.ds(start, width)], xt.at[k], load_sem.at[k])
         load.start()
-        loads.append(load)
 
     base = jnp.concatenate(
         [load_ref[...].astype(jnp.float32), jnp.zeros((deep - components, genes), jnp.float32)], axis=0
@@ -186,15 +184,22 @@
     weights[0] = base.astype(jnp.bfloat16)
 
     def project(k):
-        loads[k].wait()
+        pltpu.make_async_copy(target_hbm.at[:, pl.ds(0, width)], xt.at[k], load_sem.at[k]).wait()
         return proj(weights[0], xt[k])[:high]
 
-    for k in range(nz):
-        zz = along(plan[k][0])
+    def x_step(k):
+        zz = along(nz - 1 - k)
+        return remote(part_t.at[k], recv_x.at[zz], rx_send.at[k], rx_recv.at[zz], beside, core)
+
+    def z_step(d):
+        return remote(sum_t.at[d], recv_t.at[z], rt_send.at[d], rt_recv.at[z], 2 * along(d) + x, core)
+
+    pl.semaphore_wait(barrier, n)
+
+    @pl.loop(0, nz)
+    def _(k):
         part_t[k] = project(k)
-        if k == 0:
-            pl.semaphore_wait(barrier, n)
-        go(remote(part_t.at[k], recv_x.at[zz], rx_send.at[k], rx_recv.at[zz], beside, core))
+        x_step(k).start()
 
     for copy in small:
         copy.wait()
@@ -213,16 +218,21 @@
         p = peer(d)
         go(remote(part_s.at[pl.ds(pl.multiple_of(p * 8, 8), 8)], recv_s.at[me], rs_send.at[d], rs_recv.at[me], p, core))
 
-    for k in range(nz, n):
-        d, s = plan[k]
+    @pl.loop(0, nz)
+    def _(k):
+        d = nz - 1 - k
         zz = along(d)
-        block = project(k)
-        remote(recv_x.at[zz], recv_x.at[zz], rx_send.at[k - nz], rx_recv.at[zz], beside, core).wait_recv()
+        block = project(nz + k)
+        remote(recv_x.at[zz], recv_x.at[zz], rx_send.at[k], rx_recv.at[zz], beside, core).wait_recv()
         block = block + recv_x[zz]
-        if d:
+
+        @pl.when(d > 0)
+        def _():
             sum_t[d] = block
-            go(remote(sum_t.at[d], recv_t.at[z], rt_send.at[d], rt_recv.at[z], s, core))
-        else:
+            z_step(d).start()
+
+        @pl.when(d == 0)
+        def _():
             recv_t[z] = block
 
     for d in turn:
@@ -390,6 +400,10 @@
         out_ref[:, lanes(t)] = own_u * kern[mine_rows, lanes(t)] * col_v[:, lanes(t)]
     for copy in sends:
         copy.wait_send()
+    for k in range(nz):
+        x_step(k).wait_send()
+        if k:
+            z_step(k).wait_send()
     for k in range(1, n):
         if k < nz:
             by_x(k).wait_send()

time: 42.3 us -> 41.7 us (0.986)
  Pallas kernels: 40.2 us -> 39.6 us
    pallas_call x1, Pallas kernels: 40.2 us -> 39.6 us  [fused_call(): pl.pallas_call(functools.partial(fused, n), out_shape=jax.ShapeDtypeStruc...]
where the time goes in v4:
time: 41.7 us; the launch traced here: 41.5 us
  Pallas kernels  39.6 us (95%)
  local copies, waits for them, and re-layouts  1.87 us (4%)
    pallas_call x1, Pallas kernels, fused_call(): pl.pallas_call(functools.partial(fused, n), out_shape=jax.ShapeDtypeStruc...  39.6 us
    unnamed x1, local copies, waits for them, and re-layouts  1.87 us

profile of v4, /device:TPU:0, one launch (start us, length us, event | category | flops | bytes accessed | tf_op | source)
XLA Modules:
  0.0 41.5 jit_solution(7734724565695087530)
XLA Ops:
  0.0 39.6 %shard_map.64 = f32[64,2048]{1,0:T(8,128)} custom-call(bf16[2560,512]{1,0:T(8,128)(2,1)} %source_hbm.1, bf16[2560,4096]{1,0:T(8,128)(2,1)} %target_hbm.1, bf16[50,2560]{1,0:T(8,128)(2,1)} %bitcast.4, s32[1,96]{1,0:T(1,128)} %bitcast.6, s32[1,64]{1,0:T(1,128)} %bitcast.7, s32[1,4096]{1,0:T(1,128)} %bitcast.5), custom_call_target="tpu_custom_call" | custom-call | tf_op jit(solution)/shard_map/pallas_call | solution.py:424
  39.6 1.9 %copy.8 = f32[64,2048]{1,0:T(8,128)} copy(f32[64,2048]{1,0:T(8,128)} %shard_map.64) | data formatting | bytes 1048576
